TPU v7x, 32 devices: a whole 2x2x4 slice. The times are simulated.
32 devices in a mesh: wide: 8 (over z, y), narrow: 4 (over x, core).
Axes of the slice: x: 2, y: 2, z: 4, core: 2. Of those that a mesh axis runs over, the one named last changes fastest.
Arguments:
- tokens: bfloat16 [98304, 768], P(('wide', 'narrow')), may hold values from -6 to 6
- labels: int32 [96], P(('wide', 'narrow')), may hold values from 0 to 2
- qkv_weight: bfloat16 [768, 2304], replicated, may hold values from -0.21875 to 0.21875
- out_weight: bfloat16 [768, 768], replicated, may hold values from -1.75 to 1.75
- up_weight: bfloat16 [768, 3072], replicated, may hold values from -0.21875 to 0.21875
- down_weight: bfloat16 [3072, 768], replicated, may hold values from -0.109375 to 0.109375
- ffn_bias: float32 [3072], replicated, may hold values from -4 to 4
- layer_biases: float32 [6, 768], replicated, may hold values from -4 to 4
- norm_gains: float32 [2, 768], replicated, may hold values from 0.5 to 1.5
- pool_weight: float32 [768, 768], replicated, may hold values from -0.21875 to 0.21875
- pool_moment: float32 [768, 768], replicated, may hold values from -3 to 3
- class_weight: float32 [768, 3], replicated, may hold values from -0.21875 to 0.21875
- class_moment: float32 [768, 3], replicated, may hold values from -20 to 20
- ramp_biases: float32 [771], replicated, may hold values from -3 to 3
- bias_moment: float32 [771], replicated, may hold values from -6 to 6
- start_factor: float32 [768, 8], replicated, may hold values from -6 to 6
- error_buffer: float32 [24576, 768], P(('wide', 'narrow')), may hold values from -0.75 to 0.75
Outputs:
- layer_out: bfloat16 [98304, 768], P(('wide', 'narrow'))
- pool_moment_new: float32 [768, 768], replicated
- pool_weight_new: float32 [768, 768], replicated
- class_moment_new: float32 [768, 3], replicated
- class_weight_new: float32 [768, 3], replicated
- bias_moment_new: float32 [771], replicated
- ramp_biases_new: float32 [771], replicated
- error_new: float32 [24576, 768], P(('wide', 'narrow'))
- factor_new: float32 [768, 8], replicated
All inputs are finite; a program needn't handle non-finite values.
Results may differ from a plain program's by a relative error of at most 0.012.
Values sent between devices are 32-bit elements; how exact they have to be, the bound alone decides.
A program may use at most 192 MiB of HBM per device.

v0:
```python
import functools

import jax
import jax.numpy as jnp
from jax import lax
from jax.experimental import pallas as pl
from jax.experimental.pallas import tpu as pltpu
from jax.sharding import PartitionSpec as P

HEAD_DIM = 64
SEQ_LEN = 1024
PAIR = 128
V_ROWS = 80
ROW_TILE = 16
LANES = 128
BLOCK = 512
LOG2E = 1.4426950408889634
SAFE = 2.0**100
MOMENTUM = 0.9
RATE_POOL = 0.03
RATE_HEAD = 0.002
RATE_BIAS = 0.03
VMEM_BYTES = 60 * 1024 * 1024

f32 = jnp.float32
bf16 = jnp.bfloat16
NT = ((1,), (1,))
TN = ((0,), (0,))


def dot(left, right, contract=((1,), (0,)), precision=None):
    return lax.dot_general(
        left, right, (contract, ((), ())), precision=precision, preferred_element_type=f32
    )


dot_full = functools.partial(dot, precision=lax.Precision.HIGHEST)


def norm_rows(values, gain, shift):
    centred = values - jnp.mean(values, -1, keepdims=True)
    variance = jnp.mean(centred * centred, -1, keepdims=True)
    return centred * lax.rsqrt(variance + 1e-12) * gain + shift


def gelu(values):
    half = 0.5 * values
    return half * lax.erf(values * 0.7071067811865476) + half


def head_sums(scores, values_aug, shifted):
    if shifted:
        scores = scores - jnp.max(scores, 0, keepdims=True)
    return dot(values_aug, jnp.exp2(scores * LOG2E).astype(bf16))


def put_context(context_t, head, sums):
    scale = 1.0 / sums[HEAD_DIM : HEAD_DIM + 8]
    groups = [sums[g : g + 8] * scale for g in range(0, HEAD_DIM, 8)]
    rows = pl.ds(pl.multiple_of(head * HEAD_DIM, HEAD_DIM), HEAD_DIM)
    context_t[rows, :] = jnp.concatenate(groups, 0).astype(bf16)


def attention_kernel(
    unroll,
    tokens,
    qkv_weight,
    layer_biases,
    context,
    first_context,
    first_tokens,
    query_weight_t,
    value_weight_t,
    query_bias,
    value_bias,
    keys,
    queries_t,
    values_t,
    context_t,
    low,
    high,
):
    length, width = tokens.shape
    heads = width // HEAD_DIM

    @pl.when(pl.program_id(0) == 0)
    def _():
        query_weight_t[...] = qkv_weight[:, :width].T
        value_weight_t[...] = qkv_weight[:, 2 * width :].T
        columns = jnp.concatenate([layer_biases[...], jnp.zeros((2, width), f32)], 0).T
        query_bias[...] = jnp.broadcast_to(columns[:, 0:1], (width, LANES))
        value_bias[...] = jnp.broadcast_to(columns[:, 1:2], (width, LANES))
        queries_t[...] = jnp.zeros_like(queries_t)
        values_t[:, HEAD_DIM:, :] = jnp.ones((heads, V_ROWS - HEAD_DIM, length), bf16)

    def wide_bias(bias):
        return jnp.concatenate([bias[...]] * (length // LANES), 1)

    sequence = tokens[...]
    key_rows = dot(sequence, qkv_weight[:, width : 2 * width]).astype(bf16)
    for pair in range(heads // 2):
        keys[pair] = key_rows[:, pair * PAIR : (pair + 1) * PAIR]
    query_cols = (dot(query_weight_t[...], sequence, NT) + wide_bias(query_bias)).astype(bf16)
    query_cols = query_cols * jnp.bfloat16(1.0 / HEAD_DIM**0.5)
    value_cols = (dot(value_weight_t[...], sequence, NT) + wide_bias(value_bias)).astype(bf16)
    for head in range(heads):
        own = slice(head * HEAD_DIM, (head + 1) * HEAD_DIM)
        half = (head % 2) * HEAD_DIM
        queries_t[head, half : half + HEAD_DIM, :] = query_cols[own]
        values_t[head, :HEAD_DIM, :] = value_cols[own]

    low[...] = jnp.ones_like(low)
    high[...] = jnp.ones_like(high)

    @pl.loop(0, heads // unroll)
    def _(group):
        for offset in range(unroll):
            head = group * unroll + offset
            sums = head_sums(dot(keys[head // 2], queries_t[head]), values_t[head], False)
            denominators = sums[HEAD_DIM : HEAD_DIM + 8]
            low[...] = jnp.minimum(low[...], denominators)
            high[...] = jnp.maximum(high[...], denominators)
            put_context(context_t, head, sums)

    in_range = (jnp.min(low[...]) > 1.0 / SAFE) & (jnp.max(high[...]) < SAFE)

    @pl.when(jnp.logical_not(in_range))
    def _():
        @pl.loop(0, heads)
        def _(head):
            sums = head_sums(dot(keys[head // 2], queries_t[head]), values_t[head], True)
            put_context(context_t, head, sums)

    done = context_t[...].T
    context[...] = done
    first_context[...] = done[:ROW_TILE]
    first_tokens[...] = sequence[:ROW_TILE]


def attention(tokens, qkv_weight, layer_biases):
    rows, width = tokens.shape
    count = rows // SEQ_LEN
    heads = width // HEAD_DIM
    by_sequence = lambda i: (i, 0)
    whole = lambda i: (0, 0)
    return pl.pallas_call(
        functools.partial(attention_kernel, 3),
        grid=(count,),
        in_specs=[
            pl.BlockSpec((SEQ_LEN, width), by_sequence),
            pl.BlockSpec((width, 3 * width), whole, pipeline_mode=pl.Buffered(1)),
            pl.BlockSpec((6, width), whole),
        ],
        out_specs=[
            pl.BlockSpec((SEQ_LEN, width), by_sequence),
            pl.BlockSpec((ROW_TILE, width), by_sequence),
            pl.BlockSpec((ROW_TILE, width), by_sequence),
        ],
        out_shape=[
            jax.ShapeDtypeStruct((rows, width), bf16),
            jax.ShapeDtypeStruct((ROW_TILE * count, width), bf16),
            jax.ShapeDtypeStruct((ROW_TILE * count, width), bf16),
        ],
        scratch_shapes=[
            pltpu.VMEM((width, width), bf16),
            pltpu.VMEM((width, width), bf16),
            pltpu.VMEM((width, LANES), f32),
            pltpu.VMEM((width, LANES), f32),
            pltpu.VMEM((heads // 2, SEQ_LEN, PAIR), bf16),
            pltpu.VMEM((heads, PAIR, SEQ_LEN), bf16),
            pltpu.VMEM((heads, V_ROWS, SEQ_LEN), bf16),
            pltpu.VMEM((width, SEQ_LEN), bf16),
            pltpu.VMEM((8, SEQ_LEN), f32),
            pltpu.VMEM((8, SEQ_LEN), f32),
        ],
        compiler_params=pltpu.CompilerParams(vmem_limit_bytes=VMEM_BYTES),
        name="attention",
    )(tokens, qkv_weight, layer_biases)


def layer_tail(tokens, context, out_weight, up_weight, down_weight, ffn_bias, biases, gains):
    attended = dot(context, out_weight) + biases[2:3]
    middle = norm_rows(tokens.astype(f32) + attended, gains[0:1], biases[3:4]).astype(bf16)
    hidden = gelu(dot(middle, up_weight) + ffn_bias).astype(bf16)
    branch = dot(hidden, down_weight) + biases[4:5]
    return norm_rows(middle.astype(f32) + branch, gains[1:2], biases[5:6]).astype(bf16)


def orthonormal_rows(factor):
    index = lax.broadcasted_iota(jnp.int32, factor.shape, 0)
    for row in range(factor.shape[0]):
        vector = factor[row : row + 1]
        vector = vector * lax.rsqrt(jnp.sum(vector * vector, -1, keepdims=True) + 1e-06)
        along = jnp.sum(factor * vector, -1, keepdims=True)
        factor = jnp.where(index > row, factor - along * vector, factor)
        factor = jnp.where(index == row, vector, factor)
    return factor


def exchange(slots, send_sem, recv_sem, value, me, count, device_of):
    slots[me] = value
    copies = []
    for step in range(1, count):
        copy = pltpu.make_async_remote_copy(
            src_ref=slots.at[me],
            dst_ref=slots.at[me],
            send_sem=send_sem.at[step],
            recv_sem=recv_sem.at[me],
            device_id=device_of(lax.rem(me + step, count)),
            device_id_type=pl.DeviceIdType.MESH,
        )
        copy.start()
        copies.append(copy)
    for step in range(1, count):
        source = lax.rem(me + count - step, count)
        pltpu.make_async_remote_copy(
            src_ref=slots.at[source],
            dst_ref=slots.at[source],
            send_sem=send_sem.at[step],
            recv_sem=recv_sem.at[source],
            device_id=device_of(source),
            device_id_type=pl.DeviceIdType.MESH,
        ).wait_recv()
    for copy in copies:
        copy.wait_send()
    total = slots[0]
    for other in range(1, count):
        total = total + slots[other]
    return total


def ramp_kernel(
    n_wide,
    n_narrow,
    labels,
    first_tokens,
    first_context,
    out_weight,
    up_weight,
    down_weight,
    ffn_bias,
    layer_biases,
    norm_gains,
    pool_weight,
    class_weight_t,
    ramp_biases,
    start_t,
    error,
    basis_out,
    factor_out,
    head_out,
    rows_out,
    grads_out,
    bias_row,
    narrow_one,
    wide_one,
    narrow_two,
    wide_two,
    send_sem,
    recv_sem,
):
    wide, narrow = lax.axis_index("wide"), lax.axis_index("narrow")
    width = error.shape[1]
    rank = start_t.shape[0]
    classes = class_weight_t.shape[0]
    rows = first_tokens.shape[0]

    along_narrow = lambda other: (wide, other)
    along_wide = lambda other: (other, narrow)

    barrier = pltpu.get_barrier_semaphore()
    for step in range(1, n_narrow):
        pl.semaphore_signal(
            barrier,
            inc=1,
            device_id=along_narrow(lax.rem(narrow + step, n_narrow)),
            device_id_type=pl.DeviceIdType.MESH,
        )
    for step in range(1, n_wide):
        pl.semaphore_signal(
            barrier,
            inc=1,
            device_id=along_wide(lax.rem(wide + step, n_wide)),
            device_id_type=pl.DeviceIdType.MESH,
        )
    pl.semaphore_wait(barrier, n_narrow + n_wide - 2)

    bias_row[...] = jnp.zeros_like(bias_row)
    bias_row[:, : width + classes] = ramp_biases[...]

    first_rows = layer_tail(
        first_tokens[...],
        first_context[...],
        out_weight[...],
        up_weight[...],
        down_weight[...],
        ffn_bias[...],
        layer_biases[...],
        norm_gains[...],
    )
    class_low = jnp.concatenate(
        [class_weight_t[...], jnp.zeros((LANES - classes, width), f32)], 0
    ).astype(bf16)
    pre = dot(first_rows, pool_weight[...].astype(bf16)) + bias_row[:, :width]
    pooled = jnp.tanh(pre)
    pooled_low = pooled.astype(bf16)
    logits = dot(pooled_low, class_low, NT) + bias_row[:, width:]
    lane = lax.broadcasted_iota(jnp.int32, logits.shape, 1)
    row = lax.broadcasted_iota(jnp.int32, logits.shape, 0)
    target = jnp.full(logits.shape, -1, jnp.int32)
    for index in range(rows // ROW_TILE):
        target = jnp.where(row == index * ROW_TILE, labels[index], target)
    logits = jnp.where(lane < classes, logits, -jnp.inf)
    powers = jnp.exp(logits - jnp.max(logits, -1, keepdims=True))
    softened = powers / jnp.sum(powers, -1, keepdims=True)
    grad_logits = softened - (lane == target).astype(f32)
    grad_logits = jnp.where(row % ROW_TILE == 0, grad_logits, 0.0).astype(bf16)
    grad_class = dot(grad_logits, pooled_low, TN)[:8]
    grad_pooled = dot(grad_logits, class_low)
    grad_pre = (grad_pooled * (1.0 - pooled * pooled)).astype(bf16)
    rows_wide = first_rows.astype(f32)
    grads_wide = grad_pre.astype(f32)
    bias_sum = jnp.sum(grads_wide, 0, keepdims=True)
    logit_sum = jnp.concatenate(
        [
            jnp.sum(grad_logits.astype(f32), 0, keepdims=True),
            jnp.zeros((1, width - LANES), f32),
        ],
        1,
    )
    index = lax.broadcasted_iota(jnp.int32, grad_class.shape, 0)
    head = jnp.where(index == classes, bias_sum, grad_class)
    head = jnp.where(index == classes + 1, logit_sum, head)

    factor = dot_full(start_t[...], error[...], NT)
    factor = factor + dot_full(dot_full(start_t[...], grads_wide, NT), rows_wide)

    total = exchange(
        narrow_one,
        send_sem.at[0],
        recv_sem.at[0],
        jnp.concatenate([factor, head], 0),
        narrow,
        n_narrow,
        along_narrow,
    )
    total = exchange(
        wide_one, send_sem.at[1], recv_sem.at[1], total, wide, n_wide, along_wide
    )
    head_out[...] = total[rank:]
    basis = orthonormal_rows(total[:rank])
    basis_out[...] = basis
    factor = dot_full(basis, error[...])
    factor = factor + dot_full(dot_full(basis, rows_wide, NT), grads_wide)
    factor = exchange(
        narrow_two, send_sem.at[2], recv_sem.at[2], factor, narrow, n_narrow, along_narrow
    )
    factor_out[...] = exchange(
        wide_two, send_sem.at[3], recv_sem.at[3], factor, wide, n_wide, along_wide
    )
    rows_out[...] = first_rows
    grads_out[...] = grad_pre


def ramp(n_wide, n_narrow, labels, *operands):
    first_tokens = operands[0]
    start_t = operands[11]
    rank, width = start_t.shape
    rows = first_tokens.shape[0]
    most = max(n_wide, n_narrow)
    vmem = pl.BlockSpec(memory_space=pltpu.VMEM)
    return pl.pallas_call(
        functools.partial(ramp_kernel, n_wide, n_narrow),
        in_specs=[pl.BlockSpec(memory_space=pltpu.SMEM)] + [vmem] * len(operands),
        out_specs=[vmem] * 5,
        out_shape=[
            jax.ShapeDtypeStruct((rank, width), f32),
            jax.ShapeDtypeStruct((rank, width), f32),
            jax.ShapeDtypeStruct((8, width), f32),
            jax.ShapeDtypeStruct((rows, width), bf16),
            jax.ShapeDtypeStruct((rows, width), bf16),
        ],
        scratch_shapes=[
            pltpu.VMEM((1, width + LANES), f32),
            pltpu.VMEM((n_narrow, rank + 8, width), f32),
            pltpu.VMEM((n_wide, rank + 8, width), f32),
            pltpu.VMEM((n_narrow, rank, width), f32),
            pltpu.VMEM((n_wide, rank, width), f32),
            pltpu.SemaphoreType.DMA((4, most)),
            pltpu.SemaphoreType.DMA((4, most)),
        ],
        compiler_params=pltpu.CompilerParams(
            vmem_limit_bytes=VMEM_BYTES, collective_id=0, has_side_effects=True
        ),
        name="ramp",
    )(labels, *operands)


def finish_kernel(
    devices,
    tokens,
    context,
    out_weight,
    up_weight,
    down_weight,
    ffn_bias,
    layer_biases,
    norm_gains,
    basis_part,
    factor,
    rows_part,
    grads,
    head,
    error,
    pool_weight,
    pool_moment,
    class_weight_t,
    class_moment_t,
    ramp_biases,
    bias_moment,
    layer_out,
    error_new,
    pool_weight_new,
    pool_moment_new,
    class_weight_new,
    class_moment_new,
    ramp_biases_new,
    bias_moment_new,
):
    width = tokens.shape[1]
    classes = class_weight_t.shape[0]
    layer_out[...] = layer_tail(
        tokens[...],
        context[...],
        out_weight[...],
        up_weight[...],
        down_weight[...],
        ffn_bias[...],
        layer_biases[...],
        norm_gains[...],
    )
    approx = dot_full(basis_part[...], factor[...], TN)
    combined = dot(rows_part[...], grads[...], TN) + error[...]
    error_new[...] = combined - approx / devices
    moment = MOMENTUM * pool_moment[...] + approx
    pool_moment_new[...] = moment
    pool_weight_new[...] = pool_weight[...] - RATE_POOL * moment

    @pl.when(pl.program_id(0) == 0)
    def _():
        moment = MOMENTUM * class_moment_t[...] + head[:classes]
        class_moment_new[...] = moment
        class_weight_new[...] = class_weight_t[...] - RATE_HEAD * moment
        total = jnp.concatenate(
            [head[classes : classes + 1], head[classes + 1 : classes + 2, :classes]], 1
        )
        moment = MOMENTUM * bias_moment[...] + total
        bias_moment_new[...] = moment
        ramp_biases_new[...] = ramp_biases[...] - RATE_BIAS * moment


def finish(devices, *operands):
    rows, width = operands[0].shape
    steps = rows // BLOCK
    part = width // steps
    once = pl.Buffered(1)
    by_rows = pl.BlockSpec((BLOCK, width), lambda i: (i, 0))
    by_part = pl.BlockSpec((part, width), lambda i: (i, 0))
    by_lanes = lambda array: pl.BlockSpec((array.shape[0], part), lambda i: (0, i))
    whole = lambda array: pl.BlockSpec(array.shape, lambda i: (0, 0), pipeline_mode=once)
    kinds = "tthhhhhhlhlhhpppwwww"
    specs = []
    for kind, operand in zip(kinds, operands, strict=True):
        if kind == "t":
            specs.append(by_rows)
        elif kind == "p":
            specs.append(by_part)
        elif kind == "l":
            specs.append(by_lanes(operand))
        else:
            specs.append(whole(operand))
    like = lambda array: jax.ShapeDtypeStruct(array.shape, array.dtype)
    small = lambda array: pl.BlockSpec(array.shape, lambda i: (0, 0))
    error, pool_weight, pool_moment = operands[13:16]
    rest = operands[16:20]
    return pl.pallas_call(
        functools.partial(finish_kernel, devices),
        grid=(steps,),
        in_specs=specs,
        out_specs=[by_rows, by_part, by_part, by_part] + [small(a) for a in rest],
        out_shape=[
            like(a) for a in (operands[0], error, pool_weight, pool_moment, *rest)
        ],
        compiler_params=pltpu.CompilerParams(vmem_limit_bytes=VMEM_BYTES),
        name="finish",
    )(*operands)


def body(
    n_wide,
    n_narrow,
    tokens,
    labels,
    qkv_weight,
    out_weight,
    up_weight,
    down_weight,
    ffn_bias,
    layer_biases,
    norm_gains,
    pool_weight,
    pool_moment,
    class_weight,
    class_moment,
    ramp_biases,
    bias_moment,
    start_factor,
    error_buffer,
):
    ffn_row = ffn_bias.reshape(1, -1)
    ramp_row = ramp_biases.reshape(1, -1)
    moment_row = bias_moment.reshape(1, -1)
    context, first_context, first_tokens = attention(tokens, qkv_weight, layer_biases)
    basis, factor, head, first_rows, grads = ramp(
        n_wide,
        n_narrow,
        labels,
        first_tokens,
        first_context,
        out_weight,
        up_weight,
        down_weight,
        ffn_row,
        layer_biases,
        norm_gains,
        pool_weight,
        class_weight.T,
        ramp_row,
        start_factor.T,
        error_buffer,
    )
    (
        layer_out,
        error_new,
        pool_weight_new,
        pool_moment_new,
        class_weight_new,
        class_moment_new,
        ramp_biases_new,
        bias_moment_new,
    ) = finish(
        n_wide * n_narrow,
        tokens,
        context,
        out_weight,
        up_weight,
        down_weight,
        ffn_row,
        layer_biases,
        norm_gains,
        basis,
        factor,
        first_rows,
        grads,
        head,
        error_buffer,
        pool_weight,
        pool_moment,
        class_weight.T,
        class_moment.T,
        ramp_row,
        moment_row,
    )
    return (
        layer_out,
        pool_moment_new,
        pool_weight_new,
        class_moment_new.T,
        class_weight_new.T,
        bias_moment_new.reshape(-1),
        ramp_biases_new.reshape(-1),
        error_new,
        factor.T,
    )


def solution(mesh):
    split = P(("wide", "narrow"), None)
    in_specs = (split, P(("wide", "narrow"))) + (P(),) * 14 + (split,)
    out_specs = (split,) + (P(),) * 6 + (split, P())
    return jax.shard_map(
        functools.partial(body, mesh.shape["wide"], mesh.shape["narrow"]),
        mesh=mesh,
        in_specs=in_specs,
        out_specs=out_specs,
        check_vma=False,
    )
```

profile of v0, /device:TPU:0, one launch (start us, length us, event | category | flops | bytes accessed | tf_op | source)
XLA Modules:
  0.0 155.7 jit_solution(18238662872195716447)
XLA Ops:
  0.6 0.0 copy-start.1
  0.7 52.4 %attention.1 = (bf16[3072,768]{1,0:T(8,128)(2,1)}, bf16[48,768]{1,0:T(8,128)(2,1)}, bf16[48,768]{1,0:T(8,128)(2,1)}) custom-call(bf16[3072,768]{1,0:T(8,128)(2,1)} %tokens.3, bf16[768,2304]{1,0:T(8,128)(2,1)} %qkv_weight.1, f32[6,768]{1,0:T(8,128)} %layer_biases.5), custom_call_target="tpu_custom_call" | custom-call | tf_op jit(solution)/shard_map/attention/pallas_call | solution.py:146
  53.0 0.0 copy-done.1
  53.0 0.6 reshape.34.ramp_biases
  53.6 0.0 copy-start.2
  53.6 45.2 %ramp.1 = (f32[8,768]{1,0:T(8,128)}, f32[8,768]{1,0:T(8,128)}, f32[8,768]{1,0:T(8,128)}, bf16[48,768]{1,0:T(8,128)(2,1)}, bf16[48,768]{1,0:T(8,128)(2,1)}) custom-call(s32[3]{0:T(128)} %labels.1, bf16[48,768]{1,0:T(8,128)(2,1)} %get-tuple-element.26.first_tokens, bf16[48,768]{1,0:T(8,128)(2,1)} %get-tuple-element.27.first_context, ...), custom_call_target="tpu_custom_call" | custom-call | tf_op jit(solution)/shard_map/ramp/pallas_call | solution.py:372
  98.8 0.0 copy-done.2
  98.8 0.6 reshape.35.bias_moment
  99.4 0.0 copy-start
  99.4 53.1 %finish.1 = (bf16[3072,768]{1,0:T(8,128)(2,1)}, f32[768,768]{1,0:T(8,128)}, f32[768,768]{1,0:T(8,128)}, f32[768,768]{1,0:T(8,128)}, f32[3,768]{1,0:T(4,128)}, /*...) custom-call(bf16[3072,768]{1,0:T(8,128)(2,1)} %tokens.3, bf16[3072,768]{1,0:T(8,128)(2,1)} %get-tuple-element.25.context, ...), custom_call_target="tpu_custom_call" | custom-call | tf_op jit(solution)/shard_map/finish/pallas_call | solution.py:486
  152.5 1.3 reduce
  153.8 1.3 reduce.1
  155.1 0.0 copy-done
  155.1 0.6 copy.27
Async XLA Ops:
  0.6 52.4 %copy-start.1 = (f32[771]{0:T(1024)S(1)}, f32[771]{0:T(1024)}, u32[]{:S(2)}) copy-start(f32[771]{0:T(1024)} %param.30) | copy-start | bytes 9256
  53.6 45.2 %copy-start.2 = (f32[771]{0:T(1024)S(1)}, f32[771]{0:T(1024)}, u32[]{:S(2)}) copy-start(f32[771]{0:T(1024)} %param.31) | copy-start | bytes 9256
  99.4 55.7 %copy-start = (f32[8,768]{1,0:T(8,128)S(1)}, f32[8,768]{1,0:T(8,128)}, u32[]{:S(2)}) copy-start(f32[8,768]{1,0:T(8,128)} %get-tuple-element.29.factor) | copy-start | bytes 73732
where the time goes:
time: 156 us
  Pallas kernels  151 us (97%)
  other arithmetic  2.58 us (2%)
  local copies, waits for them, and re-layouts  1.78 us (1%)
    pallas_call x1, Pallas kernels, finish(): pl.pallas_call(functools.partial(finish_kernel, devices), grid=(steps,),...  53.1 us
    pallas_call x1, Pallas kernels, attention(): pl.pallas_call(functools.partial(attention_kernel, 3), grid=(count,), in_...  52.4 us
    pallas_call x1, Pallas kernels, ramp(): pl.pallas_call(functools.partial(ramp_kernel, n_wide, n_narrow), in_specs...  45.2 us

commit v1 on v0

v1 whole, which is shorter than its diff:
```python
import functools

import jax
import jax.numpy as jnp
from jax import lax
from jax.experimental import pallas as pl
from jax.experimental.pallas import tpu as pltpu
from jax.sharding import PartitionSpec as P

HEAD_DIM = 64
SEQ_LEN = 1024
PAIR = 128
V_ROWS = 80
ROW_TILE = 16
LANES = 128
SLICE = 128
RAMP_STEPS = 6
LOG2E = 1.4426950408889634
SAFE = 2.0**100
MOMENTUM = 0.9
RATE_POOL = 0.03
RATE_HEAD = 0.002
RATE_BIAS = 0.03
MIB = 1024 * 1024

f32 = jnp.float32
bf16 = jnp.bfloat16
NT = ((1,), (1,))
TN = ((0,), (0,))


def dot(left, right, contract=((1,), (0,))):
    return lax.dot_general(left, right, (contract, ((), ())), preferred_element_type=f32)


def norm_rows(values, gain, shift):
    centred = values - jnp.mean(values, -1, keepdims=True)
    variance = jnp.mean(centred * centred, -1, keepdims=True)
    return centred * lax.rsqrt(variance + 1e-12) * gain + shift


def gelu(values):
    half = 0.5 * values
    return half * lax.erf(values * 0.7071067811865476) + half


def head_sums(scores, values_aug, shifted):
    if shifted:
        scores = scores - jnp.max(scores, 0, keepdims=True)
    return dot(values_aug, jnp.exp2(scores * LOG2E).astype(bf16))


def put_context(context_t, head, sums):
    scale = 1.0 / sums[HEAD_DIM : HEAD_DIM + 8]
    groups = [sums[g : g + 8] * scale for g in range(0, HEAD_DIM, 8)]
    rows = pl.ds(pl.multiple_of(head * HEAD_DIM, HEAD_DIM), HEAD_DIM)
    context_t[rows, :] = jnp.concatenate(groups, 0).astype(bf16)


def attention_kernel(
    unroll,
    tokens,
    qkv_weight,
    layer_biases,
    context,
    query_weight_t,
    value_weight_t,
    query_bias,
    value_bias,
    keys,
    queries_t,
    values_t,
    context_t,
    low,
    high,
):
    length, width = tokens.shape
    heads = width // HEAD_DIM

    @pl.when(pl.program_id(0) == 0)
    def _():
        query_weight_t[...] = qkv_weight[:, :width].T
        value_weight_t[...] = qkv_weight[:, 2 * width :].T
        columns = jnp.concatenate([layer_biases[...], jnp.zeros((2, width), f32)], 0).T
        query_bias[...] = jnp.broadcast_to(columns[:, 0:1], (width, LANES))
        value_bias[...] = jnp.broadcast_to(columns[:, 1:2], (width, LANES))
        queries_t[...] = jnp.zeros_like(queries_t)
        values_t[:, HEAD_DIM:, :] = jnp.ones((heads, V_ROWS - HEAD_DIM, length), bf16)

    def wide_bias(bias):
        return jnp.concatenate([bias[...]] * (length // LANES), 1)

    sequence = tokens[...]
    key_rows = dot(sequence, qkv_weight[:, width : 2 * width]).astype(bf16)
    for pair in range(heads // 2):
        keys[pair] = key_rows[:, pair * PAIR : (pair + 1) * PAIR]
    query_cols = (dot(query_weight_t[...], sequence, NT) + wide_bias(query_bias)).astype(bf16)
    query_cols = query_cols * jnp.bfloat16(1.0 / HEAD_DIM**0.5)
    value_cols = (dot(value_weight_t[...], sequence, NT) + wide_bias(value_bias)).astype(bf16)
    for head in range(heads):
        own = slice(head * HEAD_DIM, (head + 1) * HEAD_DIM)
        half = (head % 2) * HEAD_DIM
        queries_t[head, half : half + HEAD_DIM, :] = query_cols[own]
        values_t[head, :HEAD_DIM, :] = value_cols[own]

    low[...] = jnp.ones_like(low)
    high[...] = jnp.ones_like(high)

    @pl.loop(0, heads // unroll)
    def _(group):
        for offset in range(unroll):
            head = group * unroll + offset
            sums = head_sums(dot(keys[head // 2], queries_t[head]), values_t[head], False)
            denominators = sums[HEAD_DIM : HEAD_DIM + 8]
            low[...] = jnp.minimum(low[...], denominators)
            high[...] = jnp.maximum(high[...], denominators)
            put_context(context_t, head, sums)

    in_range = (jnp.min(low[...]) > 1.0 / SAFE) & (jnp.max(high[...]) < SAFE)

    @pl.when(jnp.logical_not(in_range))
    def _():
        @pl.loop(0, heads)
        def _(head):
            sums = head_sums(dot(keys[head // 2], queries_t[head]), values_t[head], True)
            put_context(context_t, head, sums)

    context[...] = context_t[...].T


def attention(tokens, qkv_weight, layer_biases):
    rows, width = tokens.shape
    count = rows // SEQ_LEN
    heads = width // HEAD_DIM
    by_sequence = lambda i: (i, 0)
    whole = lambda i: (0, 0)
    return pl.pallas_call(
        functools.partial(attention_kernel, 3),
        grid=(count,),
        in_specs=[
            pl.BlockSpec((SEQ_LEN, width), by_sequence),
            pl.BlockSpec((width, 3 * width), whole, pipeline_mode=pl.Buffered(1)),
            pl.BlockSpec((6, width), whole),
        ],
        out_specs=pl.BlockSpec((SEQ_LEN, width), by_sequence),
        out_shape=jax.ShapeDtypeStruct((rows, width), bf16),
        scratch_shapes=[
            pltpu.VMEM((width, width), bf16),
            pltpu.VMEM((width, width), bf16),
            pltpu.VMEM((width, LANES), f32),
            pltpu.VMEM((width, LANES), f32),
            pltpu.VMEM((heads // 2, SEQ_LEN, PAIR), bf16),
            pltpu.VMEM((heads, PAIR, SEQ_LEN), bf16),
            pltpu.VMEM((heads, V_ROWS, SEQ_LEN), bf16),
            pltpu.VMEM((width, SEQ_LEN), bf16),
            pltpu.VMEM((8, SEQ_LEN), f32),
            pltpu.VMEM((8, SEQ_LEN), f32),
        ],
        compiler_params=pltpu.CompilerParams(vmem_limit_bytes=40 * MIB),
        name="attention",
    )(tokens, qkv_weight, layer_biases)


def layer_tail(tokens, context, out_weight, up_weight, down_weight, ffn_bias, biases, gains):
    width = out_weight.shape[1]
    tokens = tokens[...].reshape(-1, width)
    attended = dot(context[...].reshape(-1, width), out_weight[...]) + biases[2:3]
    middle = norm_rows(tokens.astype(f32) + attended, gains[0:1], biases[3:4]).astype(bf16)
    ffn_row = ffn_bias[...].reshape(1, -1)
    hidden = gelu(dot(middle, up_weight[...]) + ffn_row).astype(bf16)
    branch = dot(hidden, down_weight[...]) + biases[4:5]
    return norm_rows(middle.astype(f32) + branch, gains[1:2], biases[5:6]).astype(bf16)


def orthonormal_rows(factor):
    index = lax.broadcasted_iota(jnp.int32, factor.shape, 0)
    for row in range(factor.shape[0]):
        vector = factor[row : row + 1]
        vector = vector * lax.rsqrt(jnp.sum(vector * vector, -1, keepdims=True) + 1e-06)
        along = jnp.sum(factor * vector, -1, keepdims=True)
        factor = jnp.where(index > row, factor - along * vector, factor)
        factor = jnp.where(index == row, vector, factor)
    return factor


def split(values):
    first = values.astype(bf16).astype(f32)
    second = (values - first).astype(bf16).astype(f32)
    return first, second, values - first - second


def stacked(values):
    return jnp.concatenate(split(values), 0).astype(bf16)


def folded(values):
    rows = values.shape[0] // 3
    return values[:rows] + values[rows : 2 * rows] + values[2 * rows :]


class Exchange:
    def __init__(self, slots, send_sem, recv_sem, me, count, device_of):
        self.slots, self.send_sem, self.recv_sem = slots, send_sem, recv_sem
        self.me, self.count, self.device_of = me, count, device_of

    def copy(self, step, slot, device):
        return pltpu.make_async_remote_copy(
            src_ref=self.slots.at[slot],
            dst_ref=self.slots.at[slot],
            send_sem=self.send_sem.at[step],
            recv_sem=self.recv_sem.at[slot],
            device_id=self.device_of(device),
            device_id_type=pl.DeviceIdType.MESH,
        )

    def greet(self, barrier):
        for step in range(1, self.count):
            pl.semaphore_signal(
                barrier,
                inc=1,
                device_id=self.device_of(lax.rem(self.me + step, self.count)),
                device_id_type=pl.DeviceIdType.MESH,
            )

    def start(self, value):
        self.slots[self.me] = value
        for step in range(1, self.count):
            self.copy(step, self.me, lax.rem(self.me + step, self.count)).start()

    def total(self):
        for step in range(1, self.count):
            source = lax.rem(self.me + self.count - step, self.count)
            self.copy(step, source, source).wait_recv()
            self.copy(step, self.me, lax.rem(self.me + step, self.count)).wait_send()
        total = self.slots[0]
        for other in range(1, self.count):
            total = total + self.slots[other]
        return total


def ramp_kernel(
    n_wide,
    n_narrow,
    labels,
    tokens,
    context,
    out_weight,
    up_weight,
    down_weight,
    ffn_bias,
    layer_biases,
    norm_gains,
    pool_weight,
    class_weight_t,
    ramp_biases,
    start_t,
    error,
    layer_part,
    basis_out,
    factor_out,
    head_out,
    rows_out,
    grads_out,
    bias_row,
    error_high,
    error_low,
    factor_error,
    narrow_one,
    wide_one,
    narrow_two,
    wide_two,
    send_sem,
    recv_sem,
):
    step = pl.program_id(0)
    wide, narrow = lax.axis_index("wide"), lax.axis_index("narrow")
    count = tokens.shape[0]
    width = error.shape[1]
    rank = start_t.shape[0]
    classes = class_weight_t.shape[0]

    def group(index, slots, by_narrow):
        semaphores = send_sem.at[index], recv_sem.at[index]
        if by_narrow:
            return Exchange(slots, *semaphores, narrow, n_narrow, lambda i: (wide, i))
        return Exchange(slots, *semaphores, wide, n_wide, lambda i: (i, narrow))

    sum_one_narrow = group(0, narrow_one, True)
    sum_one_wide = group(1, wide_one, False)
    sum_two_narrow = group(2, narrow_two, True)
    sum_two_wide = group(3, wide_two, False)
    barrier = pltpu.get_barrier_semaphore()

    @pl.when(step == 0)
    def _():
        sum_one_narrow.greet(barrier)
        sum_one_wide.greet(barrier)
        bias_row[...] = jnp.zeros_like(bias_row)
        bias_row[:, : width + classes] = ramp_biases[...].reshape(1, -1)
        high = error[...].astype(bf16)
        low = (error[...] - high.astype(f32)).astype(bf16)
        error_high[...] = high
        error_low[...] = low
        start = stacked(start_t[...])
        factor_error[...] = folded(dot(start, high, NT) + dot(start, low, NT))

    rows = layer_tail(
        tokens, context, out_weight, up_weight, down_weight, ffn_bias, layer_biases, norm_gains
    )
    layer_part[...] = rows.reshape(layer_part.shape)

    @pl.when(step == 0)
    def _():
        first_rows = jnp.concatenate(
            [layer_part[index, :ROW_TILE] for index in range(count)], 0
        )
        class_low = jnp.concatenate(
            [class_weight_t[...], jnp.zeros((LANES - classes, width), f32)], 0
        ).astype(bf16)
        pre = dot(first_rows, pool_weight[...].astype(bf16)) + bias_row[:, :width]
        pooled = jnp.tanh(pre)
        pooled_low = pooled.astype(bf16)
        logits = dot(pooled_low, class_low, NT) + bias_row[:, width:]
        lane = lax.broadcasted_iota(jnp.int32, logits.shape, 1)
        row = lax.broadcasted_iota(jnp.int32, logits.shape, 0)
        target = jnp.full(logits.shape, -1, jnp.int32)
        for index in range(count):
            target = jnp.where(row == index * ROW_TILE, labels[index], target)
        logits = jnp.where(lane < classes, logits, -jnp.inf)
        powers = jnp.exp(logits - jnp.max(logits, -1, keepdims=True))
        softened = powers / jnp.sum(powers, -1, keepdims=True)
        grad_logits = softened - (lane == target).astype(f32)
        grad_logits = jnp.where(row % ROW_TILE == 0, grad_logits, 0.0).astype(bf16)
        grad_class = dot(grad_logits, pooled_low, TN)[:8]
        grad_pooled = dot(grad_logits, class_low)
        grad_pre = (grad_pooled * (1.0 - pooled * pooled)).astype(bf16)
        bias_sum = jnp.sum(grad_pre.astype(f32), 0, keepdims=True)
        logit_sum = jnp.concatenate(
            [
                jnp.sum(grad_logits.astype(f32), 0, keepdims=True),
                jnp.zeros((1, width - LANES), f32),
            ],
            1,
        )
        index = lax.broadcasted_iota(jnp.int32, grad_class.shape, 0)
        head = jnp.where(index == classes, bias_sum, grad_class)
        head = jnp.where(index == classes + 1, logit_sum, head)
        inner = folded(dot(stacked(start_t[...]), grad_pre, NT))
        factor = factor_error[...] + folded(dot(stacked(inner), first_rows))
        rows_out[...] = first_rows
        grads_out[...] = grad_pre
        pl.semaphore_wait(barrier, n_narrow + n_wide - 2)
        sum_one_narrow.start(jnp.concatenate([factor, head], 0))

    @pl.when(step == 1)
    def _():
        sum_one_wide.start(sum_one_narrow.total())

    @pl.when(step == 3)
    def _():
        total = sum_one_wide.total()
        head_out[...] = total[rank:]
        basis = orthonormal_rows(total[:rank])
        basis_out[...] = basis
        basis = stacked(basis)
        inner = folded(dot(basis, rows_out[...], NT))
        factor = folded(dot(basis, error_high[...]) + dot(basis, error_low[...]))
        sum_two_narrow.start(factor + folded(dot(stacked(inner), grads_out[...])))

    @pl.when(step == 4)
    def _():
        sum_two_wide.start(sum_two_narrow.total())

    @pl.when(step == 5)
    def _():
        factor_out[...] = sum_two_wide.total()


def ramp(n_wide, n_narrow, labels, *operands):
    tokens = operands[0]
    start_t = operands[11]
    rank, width = start_t.shape
    count = tokens.shape[0]
    most = max(n_wide, n_narrow)
    block = pl.BlockSpec((count, SLICE, width), lambda i: (0, i, 0))
    vmem = pl.BlockSpec(memory_space=pltpu.VMEM)
    first = ROW_TILE * count
    return pl.pallas_call(
        functools.partial(ramp_kernel, n_wide, n_narrow),
        grid=(RAMP_STEPS,),
        in_specs=[pl.BlockSpec(memory_space=pltpu.SMEM), block, block]
        + [vmem] * (len(operands) - 2),
        out_specs=[block] + [vmem] * 5,
        out_shape=[
            jax.ShapeDtypeStruct((count, RAMP_STEPS * SLICE, width), bf16),
            jax.ShapeDtypeStruct((rank, width), f32),
            jax.ShapeDtypeStruct((rank, width), f32),
            jax.ShapeDtypeStruct((8, width), f32),
            jax.ShapeDtypeStruct((first, width), bf16),
            jax.ShapeDtypeStruct((first, width), bf16),
        ],
        scratch_shapes=[
            pltpu.VMEM((1, width + LANES), f32),
            pltpu.VMEM((width, width), bf16),
            pltpu.VMEM((width, width), bf16),
            pltpu.VMEM((rank, width), f32),
            pltpu.VMEM((n_narrow, rank + 8, width), f32),
            pltpu.VMEM((n_wide, rank + 8, width), f32),
            pltpu.VMEM((n_narrow, rank, width), f32),
            pltpu.VMEM((n_wide, rank, width), f32),
            pltpu.SemaphoreType.DMA((4, most)),
            pltpu.SemaphoreType.DMA((4, most)),
        ],
        compiler_params=pltpu.CompilerParams(
            vmem_limit_bytes=40 * MIB, collective_id=0, has_side_effects=True
        ),
        name="ramp",
    )(labels, *operands)


def finish_kernel(
    devices,
    steps,
    tokens,
    context,
    layer_part,
    out_weight,
    up_weight,
    down_weight,
    ffn_bias,
    layer_biases,
    norm_gains,
    basis_part,
    factor,
    rows_part,
    grads,
    head,
    error,
    pool_weight,
    pool_moment,
    class_weight_t,
    class_moment_t,
    ramp_biases,
    bias_moment,
    layer_out,
    error_new,
    pool_weight_new,
    pool_moment_new,
    class_weight_new,
    class_moment_new,
    ramp_biases_new,
    bias_moment_new,
    done,
    part_sem,
    done_sem,
):
    step = pl.program_id(0)
    count, _, width = tokens.shape
    classes = class_weight_t.shape[0]
    ready = layer_part.shape[1]

    part_copy = pltpu.make_async_copy(layer_part, layer_out.at[:, pl.ds(0, ready)], part_sem)

    def done_copy(index):
        where = pl.ds(ready + index * SLICE, SLICE)
        return pltpu.make_async_copy(done.at[index], layer_out.at[:, where], done_sem.at[index])

    @pl.when(step == 0)
    def _():
        part_copy.start()

    high, middle, low = split(basis_part[...])
    left = jnp.concatenate([high, high, middle, middle, high, low], 0).astype(bf16)
    high, middle, low = split(factor[...])
    right = jnp.concatenate([high, middle, high, middle, low, high], 0).astype(bf16)
    approx = dot(left, right, TN)
    combined = dot(rows_part[...], grads[...], TN) + error[...]
    error_new[...] = combined - approx * (1.0 / devices)
    moment = MOMENTUM * pool_moment[...] + approx
    pool_moment_new[...] = moment
    pool_weight_new[...] = pool_weight[...] - RATE_POOL * moment

    rows = layer_tail(
        tokens, context, out_weight, up_weight, down_weight, ffn_bias, layer_biases, norm_gains
    )
    for index in range(steps):

        @pl.when(step == index)
        def _():
            done[index] = rows.reshape(count, SLICE, width)
            done_copy(index).start()

    @pl.when(step == 0)
    def _():
        moment = MOMENTUM * class_moment_t[...] + head[:classes]
        class_moment_new[...] = moment
        class_weight_new[...] = class_weight_t[...] - RATE_HEAD * moment
        total = jnp.concatenate(
            [head[classes : classes + 1], head[classes + 1 : classes + 2, :classes]], 1
        )
        moment = MOMENTUM * bias_moment[...] + total.reshape(-1)
        bias_moment_new[...] = moment
        ramp_biases_new[...] = ramp_biases[...] - RATE_BIAS * moment

    @pl.when(step == steps - 1)
    def _():
        part_copy.wait()
        for index in range(steps):
            done_copy(index).wait()


def finish(devices, *operands):
    count, length, width = operands[0].shape
    steps = length // SLICE - RAMP_STEPS
    part = width // steps
    block = pl.BlockSpec((count, SLICE, width), lambda i: (0, i + RAMP_STEPS, 0))
    by_part = pl.BlockSpec((part, width), lambda i: (i, 0))
    vmem = pl.BlockSpec(memory_space=pltpu.VMEM)
    anywhere = pl.BlockSpec(memory_space=pl.ANY)
    specs = []
    for kind, operand in zip("bbavvvvvvlvlvvpppvvvv", operands, strict=True):
        lanes = pl.BlockSpec((operand.shape[0], part), lambda i: (0, i))
        specs.append({"b": block, "a": anywhere, "v": vmem, "l": lanes, "p": by_part}[kind])
    like = lambda array: jax.ShapeDtypeStruct(array.shape, array.dtype)
    return pl.pallas_call(
        functools.partial(finish_kernel, devices, steps),
        grid=(steps,),
        in_specs=specs,
        out_specs=[anywhere] + [by_part] * 3 + [vmem] * 4,
        out_shape=[like(operands[0])] + [like(array) for array in operands[14:21]],
        scratch_shapes=[
            pltpu.VMEM((steps, count, SLICE, width), bf16),
            pltpu.SemaphoreType.DMA,
            pltpu.SemaphoreType.DMA((steps,)),
        ],
        compiler_params=pltpu.CompilerParams(vmem_limit_bytes=40 * MIB),
        name="finish",
    )(*operands)


def body(
    n_wide,
    n_narrow,
    tokens,
    labels,
    qkv_weight,
    out_weight,
    up_weight,
    down_weight,
    ffn_bias,
    layer_biases,
    norm_gains,
    pool_weight,
    pool_moment,
    class_weight,
    class_moment,
    ramp_biases,
    bias_moment,
    start_factor,
    error_buffer,
):
    width = tokens.shape[1]
    context = attention(tokens, qkv_weight, layer_biases).reshape(-1, SEQ_LEN, width)
    sequences = tokens.reshape(-1, SEQ_LEN, width)
    layer = (out_weight, up_weight, down_weight, ffn_bias, layer_biases, norm_gains)
    layer_part, basis, factor, head, first_rows, grads = ramp(
        n_wide,
        n_narrow,
        labels,
        sequences,
        context,
        *layer,
        pool_weight,
        class_weight.T,
        ramp_biases,
        start_factor.T,
        error_buffer,
    )
    (
        layer_out,
        error_new,
        pool_weight_new,
        pool_moment_new,
        class_weight_new,
        class_moment_new,
        ramp_biases_new,
        bias_moment_new,
    ) = finish(
        n_wide * n_narrow,
        sequences,
        context,
        layer_part,
        *layer,
        basis,
        factor,
        first_rows,
        grads,
        head,
        error_buffer,
        pool_weight,
        pool_moment,
        class_weight.T,
        class_moment.T,
        ramp_biases,
        bias_moment,
    )
    return (
        layer_out.reshape(tokens.shape),
        pool_moment_new,
        pool_weight_new,
        class_moment_new.T,
        class_weight_new.T,
        bias_moment_new,
        ramp_biases_new,
        error_new,
        factor.T,
    )


def solution(mesh):
    rows = P(("wide", "narrow"), None)
    in_specs = (rows, P(("wide", "narrow"))) + (P(),) * 14 + (rows,)
    out_specs = (rows,) + (P(),) * 6 + (rows, P())
    return jax.shard_map(
        functools.partial(body, mesh.shape["wide"], mesh.shape["narrow"]),
        mesh=mesh,
        in_specs=in_specs,
        out_specs=out_specs,
        check_vma=False,
    )
```

time: 156 us -> 126 us (0.81)
  Pallas kernels: 151 us -> 117 us
  local copies, waits for them, and re-layouts: 1.78 us -> 7.85 us
  other arithmetic: 2.58 us -> 0 us
    pallas_call x2, Pallas kernels: 98.3 us -> 68.4 us  [the longest x1 48 us: ramp(): pl.pallas_call(functools.partial(ramp_kernel, n_wide, n_narrow), grid=(RA...]
    unnamed x7 -> x35, local copies, waits for them, and re-layouts: 0.62 us -> 7.85 us
    pallas_call x1, Pallas kernels: 52.4 us -> 48.7 us  [attention(): pl.pallas_call(functools.partial(attention_kernel, 3), grid=(count,), in_...]
    pallas_call x2 -> x0, other arithmetic: 2.58 us -> none  [finish(): pl.pallas_call(functools.partial(finish_kernel, devices), grid=(steps,),...]
where the time goes in v1:
time: 126 us
  Pallas kernels  117 us (93%)
  local copies, waits for them, and re-layouts  7.85 us (6%)
    pallas_call x1, Pallas kernels, attention(): pl.pallas_call(functools.partial(attention_kernel, 3), grid=(count,), in_...  48.7 us
    pallas_call x1, Pallas kernels, ramp(): pl.pallas_call(functools.partial(ramp_kernel, n_wide, n_narrow), grid=(RA...  48 us
    pallas_call x1, Pallas kernels, finish(): pl.pallas_call(functools.partial(finish_kernel, devices, steps), grid=(st...  20.5 us
    unnamed x35, local copies, waits for them, and re-layouts  7.85 us

profile of v1, /device:TPU:0, one launch (start us, length us, event | category | flops | bytes accessed | tf_op | source)
XLA Modules:
  0.0 125.9 jit_solution(7634740972197516017)
XLA Ops:
  0.6 0.0 copy-start
  0.7 2.3 %copy-done = bf16[3072,768]{1,0:T(8,128)(2,1)S(1)} copy-done((bf16[3072,768]{1,0:T(8,128)(2,1)S(1)}, bf16[3072,768]{1,0:T(8,128)(2,1)}, u32[]{:S(2)}) %copy-start) | copy-done | bytes 4718616
  3.0 0.0 copy-start.5
  3.0 2.0 %copy-done.5 = bf16[768,2304]{1,0:T(8,128)(2,1)S(1)} copy-done((bf16[768,2304]{1,0:T(8,128)(2,1)S(1)}, bf16[768,2304]{1,0:T(8,128)(2,1)}, u32[]{:S(2)}) %copy-start.5) | copy-done | bytes 3538968
  5.0 0.0 copy-start.7
  5.0 0.7 copy-done.7
  5.7 0.0 copy-start.2
  5.7 0.0 copy-start.3
  5.7 0.0 copy-start.4
  5.7 0.0 copy-start.8
  5.7 0.0 copy-start.9
  5.7 0.0 copy-start.10
  5.8 0.0 copy-start.11
  5.8 0.0 copy-start.12
  5.8 0.0 copy-start.13
  5.8 0.0 copy-start.16
  5.8 48.7 %attention.1 = bf16[3072,768]{1,0:T(8,128)(2,1)S(1)} custom-call(bf16[3072,768]{1,0:T(8,128)(2,1)S(1)} %copy-done, bf16[768,2304]{1,0:T(8,128)(2,1)S(1)} %copy-done.5, f32[6,768]{1,0:T(8,128)S(1)} %copy-done.7), custom_call_target="tpu_custom_call" | custom-call | tf_op jit(solution)/shard_map/attention/pallas_call | solution.py:137
  54.5 0.0 copy-start.1
  54.6 2.1 %copy-done.1 = bf16[3072,768]{1,0:T(8,128)(2,1)} copy-done((bf16[3072,768]{1,0:T(8,128)(2,1)}, bf16[3072,768]{1,0:T(8,128)(2,1)S(1)}, u32[]{:S(2)}) %copy-start.1) | copy-done | bytes 4718616
  56.7 0.0 copy-done.2
  56.7 0.0 copy-done.3
  56.7 0.0 copy-done.4
  56.7 0.0 copy-done.8
  56.7 0.0 copy-done.9
  56.7 0.0 copy-done.10
  56.7 0.0 copy-done.11
  56.7 0.0 copy-done.12
  56.7 0.0 copy-done.13
  56.7 0.0 copy-done.16
  56.7 0.0 copy-start.6
  56.8 0.0 copy-start.14
  56.8 0.0 copy-start.15
  56.8 48.0 %ramp.1 = (bf16[3,768,768]{2,1,0:T(8,128)(2,1)S(1)}, f32[8,768]{1,0:T(8,128)S(1)}, f32[8,768]{1,0:T(8,128)S(1)}, f32[8,768]{1,0:T(8,128)S(1)}, bf16[48,768]{1,0:T(8,128)(2,1)S(1)}, /*index=5*/bf16[48,768]{1,0:T(8,128)(2,1)S(1)}) custom-call(s32[3]{0:T(128)S(1)} %copy-done.16, bf16[3,1024,768]{2,1,0:T(8,128)(2,1)S(1)} %bitcast.10, ...), custom_call_target="tpu_custom_call" | custom-call | tf_op jit(solution)/shard_map/ramp/pallas_call | solution.py:388
  104.7 0.0 copy-done.6
  104.8 0.0 copy-done.14
  104.8 0.0 copy-done.15
  104.8 20.5 %finish.1 = (bf16[3,1024,768]{2,1,0:T(8,128)(2,1)}, f32[768,768]{1,0:T(8,128)}, f32[768,768]{1,0:T(8,128)}, f32[768,768]{1,0:T(8,128)}, f32[3,768]{1,0:T(4,128)}...) custom-call(bf16[3,1024,768]{2,1,0:T(8,128)(2,1)} %bitcast.9, bf16[3,1024,768]{2,1,0:T(8,128)(2,1)} %bitcast.12, ...), custom_call_target="tpu_custom_call" | custom-call | tf_op jit(solution)/shard_map/finish/pallas_call | solution.py:525
  125.3 0.6 copy.27
Async XLA Ops:
  0.6 2.3 %copy-start = (bf16[3072,768]{1,0:T(8,128)(2,1)S(1)}, bf16[3072,768]{1,0:T(8,128)(2,1)}, u32[]{:S(2)}) copy-start(bf16[3072,768]{1,0:T(8,128)(2,1)} %tokens.1) | copy-start | bytes 14155780
  3.0 2.0 %copy-start.5 = (bf16[768,2304]{1,0:T(8,128)(2,1)S(1)}, bf16[768,2304]{1,0:T(8,128)(2,1)}, u32[]{:S(2)}) copy-start(bf16[768,2304]{1,0:T(8,128)(2,1)} %qkv_weight.1) | copy-start | bytes 10616836
  5.0 0.7 copy-start.7
  5.7 50.9 %copy-start.2 = (f32[768,768]{1,0:T(8,128)S(1)}, f32[768,768]{1,0:T(8,128)}, u32[]{:S(2)}) copy-start(f32[768,768]{1,0:T(8,128)} %pool_weight.3) | copy-start | bytes 7077892
  5.7 50.9 %copy-start.3 = (f32[768,768]{1,0:T(8,128)S(1)}, f32[768,768]{1,0:T(8,128)}, u32[]{:S(2)}) copy-start(f32[768,768]{1,0:T(8,128)} %error.3) | copy-start | bytes 7077892
  5.7 50.9 %copy-start.4 = (bf16[768,768]{1,0:T(8,128)(2,1)S(1)}, bf16[768,768]{1,0:T(8,128)(2,1)}, u32[]{:S(2)}) copy-start(bf16[768,768]{1,0:T(8,128)(2,1)} %out_weight.3) | copy-start | bytes 3538948
  5.7 50.9 %copy-start.8 = (f32[6,768]{1,0:T(8,128)S(1)}, f32[6,768]{1,0:T(8,128)}, u32[]{:S(2)}) copy-start(f32[6,768]{1,0:T(8,128)} %layer_biases.5) | copy-start | bytes 55300
  5.7 50.9 %copy-start.9 = (f32[3072]{0:T(1024)S(1)}, f32[3072]{0:T(1024)}, u32[]{:S(2)}) copy-start(f32[3072]{0:T(1024)} %ffn_bias.3) | copy-start | bytes 36868
  5.7 50.9 %copy-start.10 = (f32[768,3]{0,1:T(4,128)S(1)}, f32[768,3]{0,1:T(4,128)}, u32[]{:S(2)}) copy-start(f32[768,3]{0,1:T(4,128)} %param.28) | copy-start | bytes 27652
  5.8 50.9 %copy-start.11 = (f32[2,768]{1,0:T(2,128)S(1)}, f32[2,768]{1,0:T(2,128)}, u32[]{:S(2)}) copy-start(f32[2,768]{1,0:T(2,128)} %norm_gains.3) | copy-start | bytes 18436
  5.8 50.9 %copy-start.12 = (f32[768,8]{0,1:T(8,128)S(1)}, f32[768,8]{0,1:T(8,128)}, u32[]{:S(2)}) copy-start(f32[768,8]{0,1:T(8,128)} %param.32) | copy-start | bytes 73732
  5.8 50.9 %copy-start.13 = (f32[771]{0:T(1024)S(1)}, f32[771]{0:T(1024)}, u32[]{:S(2)}) copy-start(f32[771]{0:T(1024)} %ramp_biases.3) | copy-start | bytes 9256
  5.8 50.9 %copy-start.16 = (s32[3]{0:T(128)S(1)}, s32[3]{0:T(128)}, u32[]{:S(2)}) copy-start(s32[3]{0:T(128)} %labels.1) | copy-start | bytes 40
  54.5 2.1 %copy-start.1 = (bf16[3072,768]{1,0:T(8,128)(2,1)}, bf16[3072,768]{1,0:T(8,128)(2,1)S(1)}, u32[]{:S(2)}) copy-start(bf16[3072,768]{1,0:T(8,128)(2,1)S(1)} %attention.1) | copy-start | bytes 14155780
  56.7 48.0 %copy-start.6 = (f32[768,768]{1,0:T(8,128)S(1)}, f32[768,768]{1,0:T(8,128)}, u32[]{:S(2)}) copy-start(f32[768,768]{1,0:T(8,128)} %pool_moment.1) | copy-start | bytes 7077892
  56.8 48.0 %copy-start.14 = (f32[768,3]{0,1:T(4,128)S(1)}, f32[768,3]{0,1:T(4,128)}, u32[]{:S(2)}) copy-start(f32[768,3]{0,1:T(4,128)} %param.29) | copy-start | bytes 27652
  56.8 48.0 %copy-start.15 = (f32[771]{0:T(1024)S(1)}, f32[771]{0:T(1024)}, u32[]{:S(2)}) copy-start(f32[771]{0:T(1024)} %bias_moment.1) | copy-start | bytes 9256

commit v2 on v1

--- a/solution.py
+++ b/solution.py
@@ -22,11 +22,18 @@
 RATE_HEAD = 0.002
 RATE_BIAS = 0.03
 MIB = 1024 * 1024
+ATTENTION_MIB = 36
+RAMP_MIB = 18
+FINISH_MIB = 18
 
 f32 = jnp.float32
 bf16 = jnp.bfloat16
 NT = ((1,), (1,))
 TN = ((0,), (0,))
+
+
+def in_hbm(array):
+    return pltpu.with_memory_space_constraint(array, pltpu.HBM)
 
 
 def dot(left, right, contract=((1,), (0,))):
@@ -57,45 +64,89 @@
     context_t[rows, :] = jnp.concatenate(groups, 0).astype(bf16)
 
 
-def attention_kernel(
-    unroll,
-    tokens,
-    qkv_weight,
-    layer_biases,
-    context,
-    query_weight_t,
-    value_weight_t,
-    query_bias,
-    value_bias,
-    keys,
-    queries_t,
-    values_t,
-    context_t,
-    low,
-    high,
-):
-    length, width = tokens.shape
+def attention_kernel(unroll, carried, tokens, qkv_weight, layer_biases, *refs):
+    sources, context, targets = refs[:carried], refs[carried], refs[carried + 1 :][:carried]
+    (
+        query_weight,
+        key_weight,
+        value_weight,
+        query_weight_t,
+        value_weight_t,
+        query_bias,
+        value_bias,
+        sequences,
+        keys,
+        queries_t,
+        values_t,
+        context_t,
+        done,
+        low,
+        high,
+        weight_sem,
+        token_sem,
+        done_sem,
+        carry_sem,
+    ) = refs[2 * carried + 1 :]
+    step = pl.program_id(0)
+    steps = pl.num_programs(0)
+    _, length, width = sequences.shape
     heads = width // HEAD_DIM
 
-    @pl.when(pl.program_id(0) == 0)
-    def _():
-        query_weight_t[...] = qkv_weight[:, :width].T
-        value_weight_t[...] = qkv_weight[:, 2 * width :].T
+    def weight_copy(index, into):
+        columns = qkv_weight.at[:, pl.ds(index * width, width)]
+        return pltpu.make_async_copy(columns, into, weight_sem.at[index])
+
+    def token_copy(index):
+        rows = tokens.at[pl.ds(pl.multiple_of(index * length, length), length)]
+        slot = lax.rem(index, 2)
+        return pltpu.make_async_copy(rows, sequences.at[slot], token_sem.at[slot])
+
+    def done_copy(index):
+        rows = context.at[pl.ds(pl.multiple_of(index * length, length), length)]
+        return pltpu.make_async_copy(done, rows, done_sem)
+
+    carries = [
+        pltpu.make_async_copy(source, target, carry_sem.at[index])
+        for index, (source, target) in enumerate(zip(sources, targets, strict=True))
+    ]
+    query_copy = weight_copy(0, query_weight)
+    key_copy = weight_copy(1, key_weight)
+    value_copy = weight_copy(2, value_weight)
+
+    @pl.when(step == 0)
+    def _():
+        query_copy.start()
+        value_copy.start()
+        token_copy(0).start()
+        key_copy.start()
         columns = jnp.concatenate([layer_biases[...], jnp.zeros((2, width), f32)], 0).T
         query_bias[...] = jnp.broadcast_to(columns[:, 0:1], (width, LANES))
         value_bias[...] = jnp.broadcast_to(columns[:, 1:2], (width, LANES))
         queries_t[...] = jnp.zeros_like(queries_t)
         values_t[:, HEAD_DIM:, :] = jnp.ones((heads, V_ROWS - HEAD_DIM, length), bf16)
+        query_copy.wait()
+        query_weight_t[...] = query_weight[...].T
+        value_copy.wait()
+        value_weight_t[...] = value_weight[...].T
+        key_copy.wait()
+        for copy in carries:
+            copy.start()
+
+    token_copy(step).wait()
+
+    @pl.when(step + 1 < steps)
+    def _():
+        token_copy(step + 1).start()
 
     def wide_bias(bias):
         return jnp.concatenate([bias[...]] * (length // LANES), 1)
 
-    sequence = tokens[...]
-    key_rows = dot(sequence, qkv_weight[:, width : 2 * width]).astype(bf16)
+    sequence = sequences[lax.rem(step, 2)]
+    key_rows = dot(sequence, key_weight[...]).astype(bf16)
     for pair in range(heads // 2):
         keys[pair] = key_rows[:, pair * PAIR : (pair + 1) * PAIR]
-    query_cols = (dot(query_weight_t[...], sequence, NT) + wide_bias(query_bias)).astype(bf16)
-    query_cols = query_cols * jnp.bfloat16(1.0 / HEAD_DIM**0.5)
+
+    query_cols = ((dot(query_weight_t[...], sequence, NT) + wide_bias(query_bias)) * 0.125).astype(bf16)
     value_cols = (dot(value_weight_t[...], sequence, NT) + wide_bias(value_bias)).astype(bf16)
     for head in range(heads):
         own = slice(head * HEAD_DIM, (head + 1) * HEAD_DIM)
@@ -125,51 +176,71 @@
             sums = head_sums(dot(keys[head // 2], queries_t[head]), values_t[head], True)
             put_context(context_t, head, sums)
 
-    context[...] = context_t[...].T
-
-
-def attention(tokens, qkv_weight, layer_biases):
+    @pl.when(step > 0)
+    def _():
+        done_copy(step - 1).wait()
+
+    done[...] = context_t[...].T
+    done_copy(step).start()
+
+    @pl.when(step == steps - 1)
+    def _():
+        for copy in carries:
+            copy.wait()
+        done_copy(step).wait()
+
+
+def attention(tokens, qkv_weight, layer_biases, carried):
     rows, width = tokens.shape
     count = rows // SEQ_LEN
     heads = width // HEAD_DIM
-    by_sequence = lambda i: (i, 0)
-    whole = lambda i: (0, 0)
+    hbm = pl.BlockSpec(memory_space=pltpu.HBM)
+    square = pltpu.VMEM((width, width), bf16)
     return pl.pallas_call(
-        functools.partial(attention_kernel, 3),
+        functools.partial(attention_kernel, 3, len(carried)),
         grid=(count,),
-        in_specs=[
-            pl.BlockSpec((SEQ_LEN, width), by_sequence),
-            pl.BlockSpec((width, 3 * width), whole, pipeline_mode=pl.Buffered(1)),
-            pl.BlockSpec((6, width), whole),
-        ],
-        out_specs=pl.BlockSpec((SEQ_LEN, width), by_sequence),
-        out_shape=jax.ShapeDtypeStruct((rows, width), bf16),
-        scratch_shapes=[
-            pltpu.VMEM((width, width), bf16),
-            pltpu.VMEM((width, width), bf16),
+        in_specs=[hbm, hbm, pl.BlockSpec((6, width), lambda i: (0, 0))] + [hbm] * len(carried),
+        out_specs=[hbm] + [pl.BlockSpec(memory_space=pltpu.VMEM)] * len(carried),
+        out_shape=[pltpu.HBM((rows, width), bf16)]
+        + [pltpu.VMEM(array.shape, array.dtype) for array in carried],
+        scratch_shapes=[square] * 5
+        + [
             pltpu.VMEM((width, LANES), f32),
             pltpu.VMEM((width, LANES), f32),
+            pltpu.VMEM((2, SEQ_LEN, width), bf16),
             pltpu.VMEM((heads // 2, SEQ_LEN, PAIR), bf16),
             pltpu.VMEM((heads, PAIR, SEQ_LEN), bf16),
             pltpu.VMEM((heads, V_ROWS, SEQ_LEN), bf16),
             pltpu.VMEM((width, SEQ_LEN), bf16),
+            pltpu.VMEM((SEQ_LEN, width), bf16),
             pltpu.VMEM((8, SEQ_LEN), f32),
             pltpu.VMEM((8, SEQ_LEN), f32),
+            pltpu.SemaphoreType.DMA((3,)),
+            pltpu.SemaphoreType.DMA((2,)),
+            pltpu.SemaphoreType.DMA,
+            pltpu.SemaphoreType.DMA((len(carried),)),
         ],
-        compiler_params=pltpu.CompilerParams(vmem_limit_bytes=40 * MIB),
+        compiler_params=pltpu.CompilerParams(vmem_limit_bytes=ATTENTION_MIB * MIB),
         name="attention",
-    )(tokens, qkv_weight, layer_biases)
-
-
-def layer_tail(tokens, context, out_weight, up_weight, down_weight, ffn_bias, biases, gains):
-    width = out_weight.shape[1]
-    tokens = tokens[...].reshape(-1, width)
-    attended = dot(context[...].reshape(-1, width), out_weight[...]) + biases[2:3]
-    middle = norm_rows(tokens.astype(f32) + attended, gains[0:1], biases[3:4]).astype(bf16)
-    ffn_row = ffn_bias[...].reshape(1, -1)
-    hidden = gelu(dot(middle, up_weight[...]) + ffn_row).astype(bf16)
-    branch = dot(hidden, down_weight[...]) + biases[4:5]
-    return norm_rows(middle.astype(f32) + branch, gains[1:2], biases[5:6]).astype(bf16)
+    )(in_hbm(tokens), in_hbm(qkv_weight), layer_biases, *[in_hbm(array) for array in carried])
+
+
+def flat(block):
+    return block[...].reshape(-1, block.shape[-1])
+
+
+def to_middle(tokens, context, out_weight, biases, gains):
+    attended = dot(flat(context), out_weight[...]) + biases[2:3]
+    return norm_rows(flat(tokens).astype(f32) + attended, gains[0:1], biases[3:4]).astype(bf16)
+
+
+def to_sums(middle, up_weight, down_weight, ffn_bias, biases):
+    hidden = gelu(dot(middle, up_weight[...]) + ffn_bias[...].reshape(1, -1)).astype(bf16)
+    return middle.astype(f32) + dot(hidden, down_weight[...]) + biases[4:5]
+
+
+def to_layer(sums, biases, gains):
+    return norm_rows(sums, gains[1:2], biases[5:6]).astype(bf16)
 
 
 def orthonormal_rows(factor):
@@ -242,6 +313,8 @@
     n_wide,
     n_narrow,
     labels,
+    first_tokens,
+    first_context,
     tokens,
     context,
     out_weight,
@@ -256,11 +329,15 @@
     start_t,
     error,
     layer_part,
+    middle,
+    sums,
     basis_out,
     factor_out,
     head_out,
     rows_out,
     grads_out,
+    next_middle,
+    next_sums,
     bias_row,
     error_high,
     error_low,
@@ -303,17 +380,24 @@
         error_low[...] = low
         start = stacked(start_t[...])
         factor_error[...] = folded(dot(start, high, NT) + dot(start, low, NT))
-
-    rows = layer_tail(
-        tokens, context, out_weight, up_weight, down_weight, ffn_bias, layer_biases, norm_gains
-    )
-    layer_part[...] = rows.reshape(layer_part.shape)
+        middle[...] = to_middle(
+            first_tokens, first_context, out_weight, layer_biases, norm_gains
+        )
+        sums[...] = jnp.zeros_like(sums)
+
+    next_middle[...] = to_middle(tokens, context, out_weight, layer_biases, norm_gains)
+    next_sums[...] = to_sums(middle[...], up_weight, down_weight, ffn_bias, layer_biases)
+    rows = to_layer(sums[...], layer_biases, norm_gains).reshape(count, SLICE, width)
+    layer_part[jnp.maximum(step - 1, 0)] = rows
+    middle[...] = next_middle[...]
+    sums[...] = next_sums[...]
 
     @pl.when(step == 0)
     def _():
-        first_rows = jnp.concatenate(
-            [layer_part[index, :ROW_TILE] for index in range(count)], 0
+        first_sums = jnp.concatenate(
+            [sums[pl.ds(index * SLICE, ROW_TILE)] for index in range(count)], 0
         )
+        first_rows = to_layer(first_sums, layer_biases, norm_gains)
         class_low = jnp.concatenate(
             [class_weight_t[...], jnp.zeros((LANES - classes, width), f32)], 0
         ).astype(bf16)
@@ -376,30 +460,38 @@
         factor_out[...] = sum_two_wide.total()
 
 
-def ramp(n_wide, n_narrow, labels, *operands):
-    tokens = operands[0]
-    start_t = operands[11]
+def ramp(n_wide, n_narrow, labels, tokens, context, *operands):
+    start_t = operands[9]
     rank, width = start_t.shape
     count = tokens.shape[0]
     most = max(n_wide, n_narrow)
-    block = pl.BlockSpec((count, SLICE, width), lambda i: (0, i, 0))
+    shape = (count, SLICE, width)
+    first_block = pl.BlockSpec(shape, lambda i: (0, 0, 0))
+    next_block = pl.BlockSpec(shape, lambda i: (0, i + 1, 0))
     vmem = pl.BlockSpec(memory_space=pltpu.VMEM)
     first = ROW_TILE * count
+    outs = [
+        pltpu.VMEM((RAMP_STEPS - 1, *shape), bf16),
+        pltpu.VMEM((count * SLICE, width), bf16),
+        pltpu.VMEM((count * SLICE, width), f32),
+        pltpu.VMEM((rank, width), f32),
+        pltpu.VMEM((rank, width), f32),
+        pltpu.VMEM((8, width), f32),
+        pltpu.VMEM((first, width), bf16),
+        pltpu.VMEM((first, width), bf16),
+    ]
     return pl.pallas_call(
         functools.partial(ramp_kernel, n_wide, n_narrow),
         grid=(RAMP_STEPS,),
-        in_specs=[pl.BlockSpec(memory_space=pltpu.SMEM), block, block]
-        + [vmem] * (len(operands) - 2),
-        out_specs=[block] + [vmem] * 5,
-        out_shape=[
-            jax.ShapeDtypeStruct((count, RAMP_STEPS * SLICE, width), bf16),
-            jax.ShapeDtypeStruct((rank, width), f32),
-            jax.ShapeDtypeStruct((rank, width), f32),
-            jax.ShapeDtypeStruct((8, width), f32),
-            jax.ShapeDtypeStruct((first, width), bf16),
-            jax.ShapeDtypeStruct((first, width), bf16),
-        ],
+        in_specs=[pl.BlockSpec(memory_space=pltpu.SMEM)]
+        + [first_block] * 2
+        + [next_block] * 2
+        + [vmem] * len(operands),
+        out_specs=[vmem] * len(outs),
+        out_shape=outs,
         scratch_shapes=[
+            pltpu.VMEM((count * SLICE, width), bf16),
+            pltpu.VMEM((count * SLICE, width), f32),
             pltpu.VMEM((1, width + LANES), f32),
             pltpu.VMEM((width, width), bf16),
             pltpu.VMEM((width, width), bf16),
@@ -412,27 +504,28 @@
             pltpu.SemaphoreType.DMA((4, most)),
         ],
         compiler_params=pltpu.CompilerParams(
-            vmem_limit_bytes=40 * MIB, collective_id=0, has_side_effects=True
+            vmem_limit_bytes=RAMP_MIB * MIB, collective_id=0, has_side_effects=True
         ),
         name="ramp",
-    )(labels, *operands)
+    )(labels, *[in_hbm(array) for array in (tokens, context, tokens, context)], *operands)
 
 
 def finish_kernel(
     devices,
-    steps,
     tokens,
     context,
     layer_part,
+    middle,
+    sums,
     out_weight,
     up_weight,
     down_weight,
     ffn_bias,
     layer_biases,
     norm_gains,
-    basis_part,
+    basis,
     factor,
-    rows_part,
+    rows,
     grads,
     head,
     error,
@@ -446,96 +539,118 @@
     error_new,
     pool_weight_new,
     pool_moment_new,
+    factor_new,
     class_weight_new,
     class_moment_new,
     ramp_biases_new,
     bias_moment_new,
+    last_tokens,
+    last_context,
     done,
+    held,
+    load_sem,
     part_sem,
     done_sem,
+    store_sem,
 ):
-    step = pl.program_id(0)
-    count, _, width = tokens.shape
+    count, length, width = tokens.shape
     classes = class_weight_t.shape[0]
-    ready = layer_part.shape[1]
-
-    part_copy = pltpu.make_async_copy(layer_part, layer_out.at[:, pl.ds(0, ready)], part_sem)
+    ready = layer_part.shape[0]
+
+    def block_of(array, index):
+        return array.at[:, pl.ds(index * SLICE, SLICE)]
+
+    parts = [
+        pltpu.make_async_copy(layer_part.at[index], block_of(layer_out, index), part_sem.at[index])
+        for index in range(ready)
+    ]
+    last = length // SLICE - 1
+    loads = [
+        pltpu.make_async_copy(block_of(source, last), into, load_sem.at[index])
+        for index, (source, into) in enumerate([(tokens, last_tokens), (context, last_context)])
+    ]
+    stores = [
+        pltpu.make_async_copy(held.at[index], into, store_sem.at[index])
+        for index, into in enumerate([error_new, pool_weight_new, pool_moment_new])
+    ]
 
     def done_copy(index):
-        where = pl.ds(ready + index * SLICE, SLICE)
-        return pltpu.make_async_copy(done.at[index], layer_out.at[:, where], done_sem.at[index])
-
-    @pl.when(step == 0)
-    def _():
-        part_copy.start()
-
-    high, middle, low = split(basis_part[...])
-    left = jnp.concatenate([high, high, middle, middle, high, low], 0).astype(bf16)
-    high, middle, low = split(factor[...])
-    right = jnp.concatenate([high, middle, high, middle, low, high], 0).astype(bf16)
+        into = block_of(layer_out, ready + index)
+        return pltpu.make_async_copy(done.at[index], into, done_sem.at[index])
+
+    def finish_block(index, values):
+        done[index] = to_layer(values, layer_biases, norm_gains).reshape(count, SLICE, width)
+        done_copy(index).start()
+
+    for copy in loads + parts:
+        copy.start()
+    finish_block(0, sums[...])
+    high, mid, low = split(basis[...])
+    left = jnp.concatenate([high, high, mid, mid, high, low], 0).astype(bf16)
+    high, mid, low = split(factor[...])
+    right = jnp.concatenate([high, mid, high, mid, low, high], 0).astype(bf16)
     approx = dot(left, right, TN)
-    combined = dot(rows_part[...], grads[...], TN) + error[...]
-    error_new[...] = combined - approx * (1.0 / devices)
+    combined = dot(rows[...], grads[...], TN) + error[...]
+    held[0] = combined - approx * (1.0 / devices)
     moment = MOMENTUM * pool_moment[...] + approx
-    pool_moment_new[...] = moment
-    pool_weight_new[...] = pool_weight[...] - RATE_POOL * moment
-
-    rows = layer_tail(
-        tokens, context, out_weight, up_weight, down_weight, ffn_bias, layer_biases, norm_gains
+    held[2] = moment
+    held[1] = pool_weight[...] - RATE_POOL * moment
+    for copy in stores:
+        copy.start()
+    factor_new[...] = factor[...]
+
+    for copy in loads:
+        copy.wait()
+    last_middle = to_middle(last_tokens, last_context, out_weight, layer_biases, norm_gains)
+    next_sums = to_sums(middle[...], up_weight, down_weight, ffn_bias, layer_biases)
+    finish_block(1, next_sums)
+    last_sums = to_sums(last_middle, up_weight, down_weight, ffn_bias, layer_biases)
+
+    moment = MOMENTUM * class_moment_t[...] + head[:classes]
+    class_moment_new[...] = moment
+    class_weight_new[...] = class_weight_t[...] - RATE_HEAD * moment
+    total = jnp.concatenate(
+        [head[classes : classes + 1], head[classes + 1 : classes + 2, :classes]], 1
     )
-    for index in range(steps):
-
-        @pl.when(step == index)
-        def _():
-            done[index] = rows.reshape(count, SLICE, width)
-            done_copy(index).start()
-
-    @pl.when(step == 0)
-    def _():
-        moment = MOMENTUM * class_moment_t[...] + head[:classes]
-        class_moment_new[...] = moment
-        class_weight_new[...] = class_weight_t[...] - RATE_HEAD * moment
-        total = jnp.concatenate(
-            [head[classes : classes + 1], head[classes + 1 : classes + 2, :classes]], 1
-        )
-        moment = MOMENTUM * bias_moment[...] + total.reshape(-1)
-        bias_moment_new[...] = moment
-        ramp_biases_new[...] = ramp_biases[...] - RATE_BIAS * moment
-
-    @pl.when(step == steps - 1)
-    def _():
-        part_copy.wait()
-        for index in range(steps):
-            done_copy(index).wait()
+    moment = MOMENTUM * bias_moment[...] + total.reshape(-1)
+    bias_moment_new[...] = moment
+    ramp_biases_new[...] = ramp_biases[...] - RATE_BIAS * moment
+
+    finish_block(2, last_sums)
+    for copy in parts + stores:
+        copy.wait()
+    for index in range(3):
+        done_copy(index).wait()
 
 
 def finish(devices, *operands):
-    count, length, width = operands[0].shape
-    steps = length // SLICE - RAMP_STEPS
-    part = width // steps
-    block = pl.BlockSpec((count, SLICE, width), lambda i: (0, i + RAMP_STEPS, 0))
-    by_part = pl.BlockSpec((part, width), lambda i: (i, 0))
+    tokens = operands[0]
+    count, length, width = tokens.shape
     vmem = pl.BlockSpec(memory_space=pltpu.VMEM)
-    anywhere = pl.BlockSpec(memory_space=pl.ANY)
-    specs = []
-    for kind, operand in zip("bbavvvvvvlvlvvpppvvvv", operands, strict=True):
-        lanes = pl.BlockSpec((operand.shape[0], part), lambda i: (0, i))
-        specs.append({"b": block, "a": anywhere, "v": vmem, "l": lanes, "p": by_part}[kind])
-    like = lambda array: jax.ShapeDtypeStruct(array.shape, array.dtype)
+    hbm = pl.BlockSpec(memory_space=pltpu.HBM)
+    layer_part, factor = operands[2], operands[12]
+    large = (tokens, *operands[16:19])
+    small = (factor, *operands[19:])
+    shape = (count, SLICE, width)
     return pl.pallas_call(
-        functools.partial(finish_kernel, devices, steps),
-        grid=(steps,),
-        in_specs=specs,
-        out_specs=[anywhere] + [by_part] * 3 + [vmem] * 4,
-        out_shape=[like(operands[0])] + [like(array) for array in operands[14:21]],
+        functools.partial(finish_kernel, devices),
+        in_specs=[hbm] * 2 + [vmem] * (len(operands) - 2),
+        out_specs=[hbm] * len(large) + [vmem] * len(small),
+        out_shape=[pltpu.HBM(array.shape, array.dtype) for array in large]
+        + [jax.ShapeDtypeStruct(array.shape, array.dtype) for array in small],
         scratch_shapes=[
-            pltpu.VMEM((steps, count, SLICE, width), bf16),
-            pltpu.SemaphoreType.DMA,
-            pltpu.SemaphoreType.DMA((steps,)),
+            pltpu.VMEM(shape, bf16),
+            pltpu.VMEM(shape, bf16),
+            pltpu.VMEM((3, *shape), bf16),
+            pltpu.VMEM((3, width, width), f32),
+            pltpu.SemaphoreType.DMA((2,)),
+            pltpu.SemaphoreType.DMA((layer_part.shape[0],)),
+            pltpu.SemaphoreType.DMA((3,)),
+            pltpu.SemaphoreType.DMA((3,)),
         ],
-        compiler_params=pltpu.CompilerParams(vmem_limit_bytes=40 * MIB),
+        compiler_params=pltpu.CompilerParams(vmem_limit_bytes=FINISH_MIB * MIB),
         name="finish",
-    )(*operands)
+    )(*[in_hbm(array) for array in operands[:2]], *operands[2:])
 
 
 def body(
@@ -560,10 +675,29 @@
     error_buffer,
 ):
     width = tokens.shape[1]
-    context = attention(tokens, qkv_weight, layer_biases).reshape(-1, SEQ_LEN, width)
+    carried = (
+        out_weight,
+        up_weight,
+        down_weight,
+        ffn_bias,
+        layer_biases,
+        norm_gains,
+        error_buffer,
+        pool_weight,
+        pool_moment,
+        class_weight.T,
+        class_moment.T,
+        ramp_biases,
+        bias_moment,
+        start_factor.T,
+    )
+    context, *carried = attention(tokens, qkv_weight, layer_biases, carried)
+    layer = carried[:6]
+    error, pool_weight, pool_moment, class_weight, class_moment = carried[6:11]
+    ramp_biases, bias_moment, start = carried[11:]
+    context = context.reshape(-1, SEQ_LEN, width)
     sequences = tokens.reshape(-1, SEQ_LEN, width)
-    layer = (out_weight, up_weight, down_weight, ffn_bias, layer_biases, norm_gains)
-    layer_part, basis, factor, head, first_rows, grads = ramp(
+    layer_part, middle, sums, basis, factor, head, first_rows, grads = ramp(
         n_wide,
         n_narrow,
         labels,
@@ -571,16 +705,17 @@
         context,
         *layer,
         pool_weight,
-        class_weight.T,
+        class_weight,
         ramp_biases,
-        start_factor.T,
-        error_buffer,
+        start,
+        error,
     )
     (
         layer_out,
         error_new,
         pool_weight_new,
         pool_moment_new,
+        factor_new,
         class_weight_new,
         class_moment_new,
         ramp_biases_new,
@@ -590,17 +725,19 @@
         sequences,
         context,
         layer_part,
+        middle,
+        sums,
         *layer,
         basis,
         factor,
         first_rows,
         grads,
         head,
-        error_buffer,
+        error,
         pool_weight,
         pool_moment,
-        class_weight.T,
-        class_moment.T,
+        class_weight,
+        class_moment,
         ramp_biases,
         bias_moment,
     )
@@ -613,7 +750,7 @@
         bias_moment_new,
         ramp_biases_new,
         error_new,
-        factor.T,
+        factor_new.T,
     )
 
 

time: 126 us -> 110 us (0.87)
  Pallas kernels: 117 us -> 108 us
  local copies, waits for them, and re-layouts: 7.85 us -> 0.01 us
    unnamed x35 -> x2, local copies, waits for them, and re-layouts: 7.85 us -> 0.01 us
    pallas_call x1, Pallas kernels: 48 us -> 42.8 us  [ramp(): pl.pallas_call(functools.partial(ramp_kernel, n_wide, n_narrow), grid=(RA...]
    pallas_call x2, Pallas kernels: 69.2 us -> 65.7 us  [the longest x1 52.2 us: attention(): pl.pallas_call(functools.partial(attention_kernel, 3, len(carried)), grid...]
where the time goes in v2:
time: 110 us; the launch traced here: 109 us
  Pallas kernels  108 us (98%)
    pallas_call x1, Pallas kernels, attention(): pl.pallas_call(functools.partial(attention_kernel, 3, len(carried)), grid...  52.2 us
    pallas_call x1, Pallas kernels, ramp(): pl.pallas_call(functools.partial(ramp_kernel, n_wide, n_narrow), grid=(RA...  42.8 us
    pallas_call x1, Pallas kernels, finish(): pl.pallas_call(functools.partial(finish_kernel, devices), in_specs=[hbm]...  13.5 us

profile of v2, /device:TPU:0, one launch (start us, length us, event | category | flops | bytes accessed | tf_op | source)
XLA Modules:
  0.0 109.3 jit_solution(3564030985579552208)
XLA Ops:
  0.6 0.0 copy-start
  0.7 52.2 %attention.1 = (bf16[3072,768]{1,0:T(8,128)(2,1)}, bf16[768,768]{1,0:T(8,128)(2,1)S(1)}, bf16[768,3072]{1,0:T(8,128)(2,1)S(1)}, bf16[3072,768]{1,0:T(8,128)(2,1)...) custom-call(bf16[3072,768]{1,0:T(8,128)(2,1)} %tokens.1, ...), custom_call_target="tpu_custom_call" | custom-call | tf_op jit(solution)/shard_map/attention/pallas_call | solution.py:199
  52.8 0.0 copy-done
  52.8 42.8 %ramp.1 = (bf16[5,3,128,768]{3,2,1,0:T(8,128)(2,1)S(1)}, bf16[384,768]{1,0:T(8,128)(2,1)S(1)}, f32[384,768]{1,0:T(8,128)S(1)}, f32[8,768]{1,0:T(8,128)S(1)}, f32...) custom-call(s32[3]{0:T(128)S(1)} %copy-done, ...), custom_call_target="tpu_custom_call" | custom-call | tf_op jit(solution)/shard_map/ramp/pallas_call | solution.py:483
  95.6 13.5 %finish.1 = (bf16[3,1024,768]{2,1,0:T(8,128)(2,1)}, f32[768,768]{1,0:T(8,128)}, f32[768,768]{1,0:T(8,128)}, f32[768,768]{1,0:T(8,128)}, f32[8,768]{1,0:T(8,128)}...) custom-call(bf16[3,1024,768]{2,1,0:T(8,128)(2,1)} %bitcast.11, ...), custom_call_target="tpu_custom_call" | custom-call | tf_op jit(solution)/shard_map/finish/pallas_call | solution.py:635
Async XLA Ops:
  0.6 52.2 %copy-start = (s32[3]{0:T(128)S(1)}, s32[3]{0:T(128)}, u32[]{:S(2)}) copy-start(s32[3]{0:T(128)} %labels.1) | copy-start | bytes 40
